TPU v7x, 128 devices: a whole 4x4x4 slice. The times are simulated.
128 devices in a mesh: tile: 16 (over x_lo, y, core), sample: 8 (over z, x_hi).
Axes of the slice: x: 4 (x_hi: 2, x_lo: 2; x = x_hi * 2 + x_lo), y: 4, z: 4, core: 2. Of those that a mesh axis runs over, the one named last changes fastest.
Arguments:
- pair: bfloat16 [256, 256, 128], P('tile', 'sample'), may hold values from -30 to 30
- pair_mask: int32 [256, 256], P('tile', 'sample'), may hold values 0 or 1
- tri_in_w: bfloat16 [128, 512], replicated, may hold values from -0.5 to 0.5
- tri_gate_w: bfloat16 [128, 128], replicated, may hold values from -0.5 to 0.5
- tri_out_w: bfloat16 [128, 128], replicated, may hold values from -0.5 to 0.5
- bias_w: bfloat16 [128, 16], replicated, may hold values from -0.5 to 0.5
- atom_feats: bfloat16 [2048, 128], P('tile'), may hold values from -6 to 6
- atom_to_token: int32 [2048], P('tile'), may hold values from 0 to 255, never falling along the last dimension, each value on 1 to 24 neighbouring positions
- atom_w: bfloat16 [128, 768], replicated, may hold values from -0.5 to 0.5
- tokens: bfloat16 [256, 256, 768], P(('tile', 'sample')), may hold values from -40 to 40
- attention_input_weight: bfloat16 [768, 3072], replicated, may hold values from -2 to 2
- attention_output_weight: bfloat16 [768, 768], replicated, may hold values from -0.21875 to 0.21875
- cot_pair: bfloat16 [256, 256, 128], P('tile', 'sample'), may hold values from -6 to 6
- token_output_cotangent: bfloat16 [256, 256, 768], P(('tile', 'sample')), may hold values from -6 to 6
Outputs:
- pair_next: float32 [256, 256, 128], P('tile', 'sample')
- token_output_rows: float32 [256, 256, 768], P(('tile', 'sample'))
- grad_pair: float32 [256, 256, 128], P('tile', 'sample')
- grad_tokens: float32 [256, 256, 768], P(('tile', 'sample'))
- grad_tri_in_w: float32 [128, 512], replicated
- grad_tri_gate_w: float32 [128, 128], replicated
- grad_tri_out_w: float32 [128, 128], replicated
- grad_bias_w: float32 [128, 16], replicated
- grad_atom_w: float32 [128, 768], replicated
- attention_input_weight_gradient: float32 [768, 3072], replicated
- attention_output_weight_gradient: float32 [768, 768], replicated
Inputs may be any that keep to these rules, and one draw needn't show every extreme that they name: `atom_to_token`: atoms are in order of their tokens; every token has 1 to 24 atoms.
All inputs are finite; a program needn't handle non-finite values. No bound on the sum of `pair_mask` on one device may be relied on, other than what follows from the above.
Results may differ from a plain program's by a relative error of at most 0.034.
Values may be sent and summed in bfloat16 or wider, within the bound.
A program may use at most 128 MiB of HBM per device.

v0:
```python
import math

import jax
import jax.numpy as jnp
from jax import lax
from jax.sharding import PartitionSpec as P

EPSILON = 1e-05
HIGHEST = lax.Precision.HIGHEST


def norm_parts(values, axis):
    centered = values - jnp.mean(values, axis=axis, keepdims=True)
    inverse = lax.rsqrt(jnp.mean(centered * centered, axis=axis, keepdims=True) + EPSILON)
    return (centered * inverse, inverse)


def norm_back(normed, inverse, incoming_gradient, axis):
    first_mean = jnp.mean(incoming_gradient, axis=axis, keepdims=True)
    second_mean = jnp.mean(incoming_gradient * normed, axis=axis, keepdims=True)
    return (incoming_gradient - first_mean - normed * second_mean) * inverse


def silu_slope(values):
    sigmoid_part = jax.nn.sigmoid(values)
    return sigmoid_part * (1.0 + values * (1.0 - sigmoid_part))


def shards(
    pair,
    pair_mask,
    tri_in_w,
    tri_gate_w,
    tri_out_w,
    bias_w,
    atom_feats,
    atom_to_token,
    atom_w,
    tokens,
    attention_input_weight,
    attention_output_weight,
    cot_pair,
    token_output_cotangent,
):
    hidden = tri_in_w.shape[1] // 4
    token_width = attention_input_weight.shape[0]
    head_count = bias_w.shape[1]
    head_size = token_width // head_count
    sample_count = tokens.shape[0]
    total_tokens = tokens.shape[1]
    score_scale = 1.0 / math.sqrt(head_size)
    pair_f = pair.astype(jnp.float32)
    normed_z, inverse_z = norm_parts(pair_f, 2)
    normed_zb = normed_z.astype(jnp.bfloat16)
    projected = jnp.einsum("ijz,zc->cij", normed_zb, tri_in_w, preferred_element_type=jnp.float32)
    mask_rows = pair_mask.astype(jnp.float32)[None]
    gate_left = jax.nn.sigmoid(projected[0:hidden])
    gate_right = jax.nn.sigmoid(projected[2 * hidden : 3 * hidden])
    left_local = (gate_left * projected[hidden : 2 * hidden] * mask_rows).astype(jnp.bfloat16)
    right_local = (gate_right * projected[3 * hidden :] * mask_rows).astype(jnp.bfloat16)
    left_panel, right_panel = (
        lax.all_to_all(left_local, "sample", split_axis=0, concat_axis=2, tiled=True),
        lax.all_to_all(right_local, "sample", split_axis=0, concat_axis=2, tiled=True),
    )
    right_all = lax.all_gather(right_panel, "tile", axis=1, tiled=True)
    product_panel = jnp.einsum(
        "cik,cjk->cij", left_panel, right_all, preferred_element_type=jnp.float32
    ).astype(jnp.bfloat16)
    product = lax.all_to_all(product_panel, "sample", split_axis=2, concat_axis=0, tiled=True)
    normed_p, inverse_p = norm_parts(product.astype(jnp.float32), 0)
    normed_pb = normed_p.astype(jnp.bfloat16)
    linear = jnp.einsum("cij,cz->ijz", normed_pb, tri_out_w, preferred_element_type=jnp.float32)
    tri_gate = jax.nn.sigmoid(
        jnp.einsum("ijz,zy->ijy", normed_zb, tri_gate_w, preferred_element_type=jnp.float32)
    )
    pair_next = pair_f + tri_gate * linear
    normed_n, inverse_n = norm_parts(pair_next, 2)
    normed_nb = normed_n.astype(jnp.bfloat16)
    bias_local = jnp.einsum(
        "ijz,zh->hij", normed_nb, bias_w, preferred_element_type=jnp.float32
    ).astype(jnp.bfloat16)
    bias_rowblock = lax.all_gather(bias_local, "sample", axis=2, tiled=True)
    bias_all = lax.all_gather(bias_rowblock, "tile", axis=1, tiled=True)
    atom_pre = jnp.dot(atom_feats, atom_w, preferred_element_type=jnp.float32)
    atom_act = jax.nn.silu(atom_pre)
    token_ids = jnp.arange(total_tokens, dtype=jnp.int32)
    one_hot = (atom_to_token[:, None] == token_ids[None, :]).astype(jnp.float32)
    sums_part = jnp.einsum("an,ad->nd", one_hot, atom_act, precision=HIGHEST)
    counts_part = jnp.sum(one_hot, axis=0)
    token_sums, token_counts = (
        lax.psum(sums_part.astype(jnp.bfloat16), "tile").astype(jnp.float32),
        lax.psum(counts_part.astype(jnp.bfloat16), "tile").astype(jnp.float32),
    )
    token_cond = token_sums / token_counts[:, None]
    token_state_rows = tokens.astype(jnp.float32) + token_cond[None]
    normed_h, inverse_h = norm_parts(token_state_rows, 2)
    normalized_hidden_bfloat = normed_h.astype(jnp.bfloat16)
    projected_hidden = jnp.einsum(
        "zut,tw->zuw",
        normalized_hidden_bfloat,
        attention_input_weight,
        preferred_element_type=jnp.float32,
    )
    queries = (
        projected_hidden[:, :, :token_width]
        .astype(jnp.bfloat16)
        .reshape(sample_count, total_tokens, head_count, head_size)
    )
    gate_values = jax.nn.sigmoid(projected_hidden[:, :, token_width : 2 * token_width])
    keys_all = (
        projected_hidden[:, :, 2 * token_width : 3 * token_width]
        .astype(jnp.bfloat16)
        .reshape(sample_count, total_tokens, head_count, head_size)
    )
    values_all = (
        projected_hidden[:, :, 3 * token_width :]
        .astype(jnp.bfloat16)
        .reshape(sample_count, total_tokens, head_count, head_size)
    )
    scores = (
        jnp.einsum("sihd,sjhd->shij", queries, keys_all, preferred_element_type=jnp.float32)
        * score_scale
        + bias_all.astype(jnp.float32)[None]
    )
    top_score = jnp.max(scores, axis=3, keepdims=True)
    weights = jnp.exp(scores - top_score)
    attn_probs = weights / jnp.sum(weights, axis=3, keepdims=True)
    probs_b = attn_probs.astype(jnp.bfloat16)
    attended = jnp.einsum(
        "shij,sjhd->sihd", probs_b, values_all, preferred_element_type=jnp.float32
    ).reshape(sample_count, total_tokens, token_width)
    gated_attention = (gate_values * attended).astype(jnp.bfloat16)
    token_output_rows = token_state_rows + jnp.einsum(
        "zut,tw->zuw", gated_attention, attention_output_weight, preferred_element_type=jnp.float32
    )
    incoming_gradient = jnp.einsum(
        "xqu,bu->xqb",
        token_output_cotangent,
        attention_output_weight,
        preferred_element_type=jnp.float32,
    )
    d_att = (incoming_gradient * gate_values).astype(jnp.bfloat16)
    d_gate = (incoming_gradient * attended * gate_values * (1.0 - gate_values)).astype(jnp.bfloat16)
    d_att_h = d_att.reshape(sample_count, total_tokens, head_count, head_size)
    d_probs = jnp.einsum("sihd,sjhd->shij", d_att_h, values_all, preferred_element_type=jnp.float32)
    d_scores = attn_probs * (d_probs - jnp.sum(attn_probs * d_probs, axis=3, keepdims=True))
    d_scores_b = d_scores.astype(jnp.bfloat16)
    d_query = (
        (
            jnp.einsum("shij,sjhd->sihd", d_scores_b, keys_all, preferred_element_type=jnp.float32)
            * score_scale
        )
        .astype(jnp.bfloat16)
        .reshape(sample_count, total_tokens, token_width)
    )
    d_key = (
        (
            jnp.einsum("shij,sihd->sjhd", d_scores_b, queries, preferred_element_type=jnp.float32)
            * score_scale
        )
        .astype(jnp.bfloat16)
        .reshape(sample_count, total_tokens, token_width)
    )
    d_value = (
        jnp.einsum("shij,sihd->sjhd", probs_b, d_att_h, preferred_element_type=jnp.float32)
        .astype(jnp.bfloat16)
        .reshape(sample_count, total_tokens, token_width)
    )
    bias_term = jnp.sum(d_scores, axis=0)
    bias_part = lax.psum_scatter(
        bias_term.astype(jnp.bfloat16), "sample", scatter_dimension=2, tiled=True
    )
    bias_grad = lax.psum_scatter(bias_part, "tile", scatter_dimension=1, tiled=True).astype(
        jnp.float32
    )
    every_gradient = jnp.concatenate([d_query, d_gate, d_key, d_value], axis=2)
    normalized_hidden_gradient = jnp.einsum(
        "xqu,bu->xqb", every_gradient, attention_input_weight, preferred_element_type=jnp.float32
    )
    attention_input_weight_gradient = jnp.einsum(
        "jol,jot->lt", normalized_hidden_bfloat, every_gradient, preferred_element_type=jnp.float32
    )
    attention_output_weight_gradient = jnp.einsum(
        "jol,jot->lt", gated_attention, token_output_cotangent, preferred_element_type=jnp.float32
    )
    grad_tokens = token_output_cotangent.astype(jnp.float32) + norm_back(
        normed_h, inverse_h, normalized_hidden_gradient, 2
    )
    token_grad_sum = lax.psum(jnp.sum(grad_tokens, axis=0), ("tile", "sample"))
    cond_grad = token_grad_sum / token_counts[:, None]
    d_act = jnp.einsum("an,nd->ad", one_hot, cond_grad, precision=HIGHEST) * silu_slope(atom_pre)
    first_copy = (lax.axis_index("sample") == 0).astype(jnp.float32)
    grad_atom_w = (
        jnp.einsum("ac,ad->cd", atom_feats.astype(jnp.float32), d_act, precision=HIGHEST)
        * first_copy
    )
    d_normed_n = jnp.einsum("hij,zh->ijz", bias_grad, bias_w.astype(jnp.float32), precision=HIGHEST)
    grad_bias_w = jnp.einsum(
        "ijz,hij->zh", normed_nb.astype(jnp.float32), bias_grad, precision=HIGHEST
    )
    d_next = cot_pair.astype(jnp.float32) + norm_back(normed_n, inverse_n, d_normed_n, 2)
    d_linear = (d_next * tri_gate).astype(jnp.bfloat16)
    d_gate_pre = (d_next * linear * tri_gate * (1.0 - tri_gate)).astype(jnp.bfloat16)
    grad_tri_out_w = jnp.einsum(
        "cij,ijz->cz", normed_pb, d_linear, preferred_element_type=jnp.float32
    )
    d_normed_p = jnp.einsum("ijz,cz->cij", d_linear, tri_out_w, preferred_element_type=jnp.float32)
    d_product = norm_back(normed_p, inverse_p, d_normed_p, 0).astype(jnp.bfloat16)
    d_product_panel = lax.all_to_all(d_product, "sample", split_axis=0, concat_axis=2, tiled=True)
    d_left_panel = jnp.einsum(
        "cij,cjk->cik", d_product_panel, right_all, preferred_element_type=jnp.float32
    ).astype(jnp.bfloat16)
    d_right_part = jnp.einsum(
        "cij,cik->cjk", d_product_panel, left_panel, preferred_element_type=jnp.float32
    )
    d_right_panel = lax.psum_scatter(
        d_right_part.astype(jnp.bfloat16), "tile", scatter_dimension=1, tiled=True
    )
    d_left, d_right = (
        lax.all_to_all(d_left_panel, "sample", split_axis=2, concat_axis=0, tiled=True),
        lax.all_to_all(d_right_panel, "sample", split_axis=2, concat_axis=0, tiled=True),
    )
    d_left_f = d_left.astype(jnp.float32)
    d_right_f = d_right.astype(jnp.float32)
    d_proj = jnp.concatenate(
        [
            d_left_f * projected[hidden : 2 * hidden] * mask_rows * gate_left * (1.0 - gate_left),
            d_left_f * gate_left * mask_rows,
            d_right_f * projected[3 * hidden :] * mask_rows * gate_right * (1.0 - gate_right),
            d_right_f * gate_right * mask_rows,
        ],
        axis=0,
    ).astype(jnp.bfloat16)
    grad_tri_in_w = jnp.einsum("ijz,cij->zc", normed_zb, d_proj, preferred_element_type=jnp.float32)
    grad_tri_gate_w = jnp.einsum(
        "ijz,ijy->zy", normed_zb, d_gate_pre, preferred_element_type=jnp.float32
    )
    d_normed_z = jnp.einsum(
        "cij,zc->ijz", d_proj, tri_in_w, preferred_element_type=jnp.float32
    ) + jnp.einsum("ijy,zy->ijz", d_gate_pre, tri_gate_w, preferred_element_type=jnp.float32)
    grad_pair = d_next + norm_back(normed_z, inverse_z, d_normed_z, 2)
    summed = tuple(
        lax.psum(
            (
                grad_tri_in_w,
                grad_tri_gate_w,
                grad_tri_out_w,
                grad_bias_w,
                grad_atom_w,
                attention_input_weight_gradient,
                attention_output_weight_gradient,
            ),
            ("tile", "sample"),
        )
    )
    return (pair_next, token_output_rows, grad_pair, grad_tokens) + summed


def solution(mesh):
    in_specs = (
        P("tile", "sample", None),
        P("tile", "sample"),
        P(),
        P(),
        P(),
        P(),
        P("tile", None),
        P("tile"),
        P(),
        P(("tile", "sample"), None, None),
        P(),
        P(),
        P("tile", "sample", None),
        P(("tile", "sample"), None, None),
    )
    out_specs = (
        P("tile", "sample", None),
        P(("tile", "sample"), None, None),
        P("tile", "sample", None),
        P(("tile", "sample"), None, None),
        P(),
        P(),
        P(),
        P(),
        P(),
        P(),
        P(),
    )
    return jax.shard_map(shards, mesh=mesh, in_specs=in_specs, out_specs=out_specs, check_vma=False)
```

profile of v0, /device:TPU:1, one launch (start us, length us, event | category | flops | bytes accessed | tf_op | source)
XLA Modules:
  0.0 878.4 jit_solution(3214622012205563880)
XLA Ops:
  12.7 15.2 %all_to_all.81 = bf16[8,2,4096]{2,1,0:T(2,128)(2,1)S(1)} all-to-all(bf16[8,2,4096]{2,1,0:T(2,128)(2,1)S(1)} %reshape.177), channel_id=1, replica_groups=mesh['tile'=16,'sample'=8] {'sample'}, dimensions={0} | all-to-all | bytes 262144 | tf_op jit(solution)/shard_map/all_to_all | solution.py:63
  42.6 20.1 %all-gather.3.cloned.1.call-done = bf16[16,256,256]{2,1,0:T(8,128)(2,1)} async-done(((bf16[16,16,256]{2,1,0:T(8,128)(2,1)}), bf16[16,256,256]{2,1,0:T(8,128)(2,1)}) %all-gather.3.cloned.1.call-update) | async-done | bytes 2097168 | tf_op jit(solution)/shard_map/all_gather | solution.py:65
  69.9 6.4 all-to-all-start.2
  77.9 5.5 all-to-all-done.2
  90.4 35.6 %all_gather.10 = bf16[16,16,256]{1,0,2:T(8,128)(2,1)} all-gather(bf16[16,16,32]{1,0,2:T(8,128)(2,1)S(1)} %copy.169), channel_id=1, replica_groups=mesh['tile'=16,'sample'=8] {'sample'}, dimensions={2}, use_global_device_ids=true | all-gather | bytes 147456 | tf_op jit(solution)/shard_map/all_gather | solution.py:82
  129.1 33.4 %psum.71 = bf16[256]{0:T(256)(128)(2,1)S(1)} all-reduce(bf16[256]{0:T(256)(128)(2,1)S(1)} %convert_reduce_fusion.1), channel_id=1, replica_groups=mesh['tile'=16,'sample'=8] {'tile'}, use_global_device_ids=true, to_apply=%region_6.7 | all-reduce | flops 256 | bytes 1024 | tf_op jit(solution)/shard_map/psum | solution.py:92
  163.0 36.2 %all-reduce.5.cloned.1.call-done = bf16[256,768]{1,0:T(8,128)(2,1)} async-done(((bf16[256,768]{1,0:T(8,128)(2,1)}), bf16[256,768]{1,0:T(8,128)(2,1)}) %all-reduce.5.cloned.1.call-update) | async-done | bytes 393232 | tf_op jit(solution)/shard_map/psum | solution.py:91
  201.1 7.0 fusion.95
  216.4 20.9 %all-gather.5.cloned.1.call-done = bf16[16,256,256]{2,0,1:T(8,128)(2,1)} async-done(((bf16[16,16,256]{2,0,1:T(8,128)(2,1)}), bf16[16,256,256]{2,0,1:T(8,128)(2,1)}) %all-gather.5.cloned.1.call-update) | async-done | bytes 2097168 | tf_op jit(solution)/shard_map/all_gather | solution.py:83
  242.2 9.6 %fusion.96 = (f32[2,16,256]{2,1,0:T(8,128)}, f32[2,16,256,256]{2,3,1,0:T(8,128)}) fusion(f32[16,256,256]{1,2,0:T(8,128)} %copy.171, bf16[2,256,16,48]{1,3,2,0:T(8,128)(2,1)} %bitcast.157, bf16[2,256,16,48]{1,3,2,0:T(8,128)(2,1)} %bitcast.159), kind=kOutput, calls=%fused_computation.159 | convolution fusion | flops 209715456 | bytes 14188544 | tf_op jit(solution)/shard_map/sub | solution.py:126
  251.8 5.5 fusion.12
  267.3 5.4 multiply_reduce_fusion
  294.1 5.8 fusion.22
  302.2 51.9 %reduce-scatter.4.cloned.1.call-done = bf16[16,256,32]{1,0,2:T(8,128)(2,1)} async-done(((bf16[16,256,256]{1,0,2:T(8,128)(2,1)}), bf16[16,256,32]{1,0,2:T(8,128)(2,1)}) %reduce-scatter.4.cloned.1.call-update) | async-done | bytes 262160 | tf_op jit(solution)/shard_map/reduce_scatter | solution.py:170
  357.4 7.1 fusion.88
  365.1 50.2 %reduce-scatter.6.cloned.1.call-done = bf16[16,16,32]{2,0,1:T(8,128)(2,1)} async-done(((bf16[16,256,32]{2,0,1:T(8,128)(2,1)}), bf16[16,16,32]{2,0,1:T(8,128)(2,1)}) %reduce-scatter.6.cloned.1.call-update) | async-done | bytes 16400 | tf_op jit(solution)/shard_map/reduce_scatter | solution.py:173
  425.7 6.8 all-to-all-start.3
  452.9 6.0 convolution_bitcast_fusion
  458.9 128.4 %all-reduce.7.cloned.1.call-done = f32[256,768]{1,0:T(8,128)} async-done(((f32[256,768]{1,0:T(8,128)}), f32[256,768]{1,0:T(8,128)}) %all-reduce.7.cloned.1.call-update) | async-done | bytes 786448 | tf_op jit(solution)/shard_map/psum | solution.py:189
  604.7 43.4 %reduce-scatter.8.cloned.1.call-done = bf16[16,16,256]{2,1,0:T(8,128)(2,1)} async-done(((bf16[16,256,256]{2,1,0:T(8,128)(2,1)}), bf16[16,16,256]{2,1,0:T(8,128)(2,1)}) %reduce-scatter.8.cloned.1.call-update) | async-done | bytes 131088 | tf_op jit(solution)/shard_map/reduce_scatter | solution.py:216
  653.9 6.6 all-to-all-start.5
  683.1 68.7 %psum.75 = f32[128,16]{0,1:T(8,128)} all-reduce(f32[128,16]{0,1:T(8,128)S(1)} %convolution_bitcast_fusion.7), channel_id=1, replica_groups=mesh['tile'=16,'sample'=8] {'tile','sample'}, use_global_device_ids=true, to_apply=%region_29.30 | all-reduce | flops 2048 | bytes 16384 | tf_op jit(solution)/shard_map/psum | solution.py:243
  755.1 99.3 %all-reduce.9.cloned.1.call-done = (f32[128,512]{1,0:T(8,128)}, f32[128,128]{1,0:T(8,128)}, f32[128,128]{1,0:T(8,128)}, f32[128,768]{0,1:T(8,128)}, f32[768,3072]{1,0:T(8,128)}, /*index=5*/f32[768,768]{1,0:T(8,128)}) async-done(((f32[128,512]{1,0:T(8,128)}, f32[128,128]{1,0:T(8,128)}, f32[128,128]{1,0:T(8,128)}, f32[128,768]{0,1:T(8,128)}, f32[768,3072]{1,0:T(8,128)}, /*index=5*/f32[768,768]{1,0:T(8,128)}), ...) | async-done | bytes 12582928 | tf_op jit(solution)/shard_map/psum | solution.py:243
  861.0 8.8 copy.214
  (242 shorter events, 179.0 us)
Async XLA Ops:
  7.2 253.2 %copy-start = (bf16[768,768]{1,0:T(8,128)(2,1)S(1)}, bf16[768,768]{1,0:T(8,128)(2,1)}, u32[]{:S(2)}) copy-start(bf16[768,768]{1,0:T(8,128)(2,1)} %param.25) | copy-start | bytes 3538948
  7.2 55.5 %all-gather.3.cloned.1.call-start = ((), (), s32[]{:S(2)}) async-start(), calls=%async_computation.9 | async-start | bytes 2228224 | tf_op jit(solution)/shard_map/all_gather | solution.py:65
  8.4 80.0 %copy-start.22 = (f32[16,32]{1,0:T(8,128)}, f32[16,32]{1,0:T(8,128)S(1)}, u32[]{:S(2)}) copy-start(f32[16,32]{1,0:T(8,128)S(1)} %broadcast_multiply_fusion.8) | copy-start | bytes 6148
  9.6 78.8 %copy-start.36 = (f32[16,32]{1,0:T(8,128)}, f32[16,32]{1,0:T(8,128)S(1)}, u32[]{:S(2)}) copy-start(f32[16,32]{1,0:T(8,128)S(1)} %add_rsqrt_fusion.2) | copy-start | bytes 6148
  31.2 10.4 %all-to-all-start = ((bf16[8,2,4096]{2,1,0:T(2,128)(2,1)}), bf16[8,2,4096]{2,1,0:T(2,128)(2,1)S(1)}, u32[]{:S(2)}, u32[]{:S(2)}) async-start(bf16[8,2,4096]{2,1,0:T(2,128)(2,1)} %reshape.175), calls=%async_computation | async-start | bytes 262144 | tf_op jit(solution)/shard_map/all_to_all | solution.py:62
  69.9 13.5 %all-to-all-start.2 = ((bf16[8,2,4096]{2,1,0:T(2,128)(2,1)}), bf16[8,2,4096]{2,1,0:T(2,128)(2,1)S(1)}, u32[]{:S(2)}, u32[]{:S(2)}) async-start(bf16[8,2,4096]{2,1,0:T(2,128)(2,1)} %reshape.179), calls=%async_computation.2 | async-start | bytes 262144 | tf_op jit(solution)/shard_map/all_to_all | solution.py:69
  76.4 122.9 %all-reduce.5.cloned.1.call-start = ((), (), s32[]{:S(2)}) async-start(), calls=%async_computation.10 | async-start | bytes 786432 | tf_op jit(solution)/shard_map/psum | solution.py:91
  77.8 159.4 %all-gather.5.cloned.1.call-start = ((), (), s32[]{:S(2)}) async-start(), calls=%async_computation.11 | async-start | bytes 2228224 | tf_op jit(solution)/shard_map/all_gather | solution.py:83
  89.5 664.2 %copy-start.3 = (f32[16,32,128]{2,1,0:T(8,128)}, f32[16,32,128]{2,1,0:T(8,128)S(1)}, u32[]{:S(2)}) copy-start(f32[16,32,128]{2,1,0:T(8,128)S(1)} %get-tuple-element.117) | copy-start | bytes 786436
  89.8 110.6 %copy-start.1 = (bf16[2,256,768]{2,1,0:T(8,128)(2,1)S(1)}, bf16[2,256,768]{2,1,0:T(8,128)(2,1)}, u32[]{:S(2)}) copy-start(bf16[2,256,768]{2,1,0:T(8,128)(2,1)} %param.23) | copy-start | bytes 2359300
  128.9 225.1 %reduce-scatter.4.cloned.1.call-start = ((), (), s32[]{:S(2)}) async-start(), calls=%async_computation.12 | async-start | bytes 2359296 | tf_op jit(solution)/shard_map/reduce_scatter | solution.py:170
  280.6 134.7 %reduce-scatter.6.cloned.1.call-start = ((), (), s32[]{:S(2)}) async-start(), calls=%async_computation.13 | async-start | bytes 1114112 | tf_op jit(solution)/shard_map/reduce_scatter | solution.py:173
  425.7 14.0 %all-to-all-start.3 = ((bf16[8,2,4096]{2,1,0:T(2,128)(2,1)}), bf16[8,2,4096]{2,1,0:T(2,128)(2,1)}, u32[]{:S(2)}, u32[]{:S(2)}) async-start(bf16[8,2,4096]{2,1,0:T(2,128)(2,1)} %reshape.181), calls=%async_computation.5 | async-start | bytes 262144 | tf_op jit(solution)/shard_map/all_to_all | solution.py:209
  432.6 154.8 %all-reduce.7.cloned.1.call-start = ((), (), s32[]{:S(2)}) async-start(), calls=%async_computation.15 | async-start | bytes 1572864 | tf_op jit(solution)/shard_map/psum | solution.py:189
  437.0 211.1 %reduce-scatter.8.cloned.1.call-start = ((), (), s32[]{:S(2)}) async-start(), calls=%async_computation.14 | async-start | bytes 2228224 | tf_op jit(solution)/shard_map/reduce_scatter | solution.py:216
  458.9 131.7 %copy-start.9 = (bf16[16,16,256]{2,1,0:T(8,128)(2,1)S(1)}, bf16[16,16,256]{2,1,0:T(8,128)(2,1)}, u32[]{:S(2)}) copy-start(bf16[16,16,256]{2,1,0:T(8,128)(2,1)} %all_to_all.72) | copy-start | bytes 393220
  597.5 56.5 %all-to-all-start.4 = ((bf16[8,2,4096]{2,1,0:T(2,128)(2,1)}), bf16[8,2,4096]{2,1,0:T(2,128)(2,1)S(1)}, u32[]{:S(2)}, u32[]{:S(2)}) async-start(bf16[8,2,4096]{2,1,0:T(2,128)(2,1)} %reshape.185), calls=%async_computation.6 | async-start | bytes 262144 | tf_op jit(solution)/shard_map/all_to_all | solution.py:220
  653.9 14.2 %all-to-all-start.5 = ((bf16[8,2,4096]{2,1,0:T(2,128)(2,1)}), bf16[8,2,4096]{2,1,0:T(2,128)(2,1)}, u32[]{:S(2)}, u32[]{:S(2)}) async-start(bf16[8,2,4096]{2,1,0:T(2,128)(2,1)} %reshape.183), calls=%async_computation.8 | async-start | bytes 262144 | tf_op jit(solution)/shard_map/all_to_all | solution.py:221
  660.5 193.9 %all-reduce.9.cloned.1.call-start = ((), (), s32[]{:S(2)}) async-start(), calls=%async_computation.16 | async-start | bytes 25165824 | tf_op jit(solution)/shard_map/psum | solution.py:243
  682.7 70.6 %copy-start.50 = (bf16[128,128]{1,0:T(8,128)(2,1)S(1)}, bf16[128,128]{1,0:T(8,128)(2,1)}, u32[]{:S(2)}) copy-start(bf16[128,128]{1,0:T(8,128)(2,1)} %param.17) | copy-start | bytes 98308
  682.8 71.0 %copy-start.8 = (f32[16,32,128]{2,1,0:T(8,128)S(1)}, f32[16,32,128]{2,1,0:T(8,128)}, u32[]{:S(2)}) copy-start(f32[16,32,128]{2,1,0:T(8,128)} %copy-done.7) | copy-start | bytes 786436
  682.8 71.0 %copy-start.17 = (bf16[16,32,128]{2,1,0:T(8,128)(2,1)S(1)}, bf16[16,32,128]{2,1,0:T(8,128)(2,1)}, u32[]{:S(2)}) copy-start(bf16[16,32,128]{2,1,0:T(8,128)(2,1)} %param.26) | copy-start | bytes 393220
  682.8 71.0 %copy-start.42 = (f32[16,32]{1,0:T(8,128)S(1)}, f32[16,32]{1,0:T(8,128)}, u32[]{:S(2)}) copy-start(f32[16,32]{1,0:T(8,128)} %copy-done.41) | copy-start | bytes 6148
  682.8 71.0 %copy-start.44 = (f32[16,32]{1,0:T(8,128)S(1)}, f32[16,32]{1,0:T(8,128)}, u32[]{:S(2)}) copy-start(f32[16,32]{1,0:T(8,128)} %copy-done.43) | copy-start | bytes 6148
  (46 other events, 535.7 us)
Sparse Core Ops, SparseCore 0:
  29.7 32.9 all-gather.2
  80.3 118.9 all-reduce.4
  201.7 35.5 all-gather.4
  280.8 73.2 reduce-scatter.3
  357.5 57.7 reduce-scatter.5
  438.3 148.9 all-reduce.6
  589.7 58.3 reduce-scatter.7
  679.8 174.6 all-reduce.8
where the time goes:
time: 888 us; the launch traced here: 878 us
  waiting for transfers between devices  464 us (52%)
  blocking collectives  153 us (17%)
  local copies, waits for them, and re-layouts  105 us (12%)
  matrix products  90.3 us (10%)
  starting transfers between devices  29.2 us (3%)
  other arithmetic  21.6 us (2%)
  between operations  15.4 us (2%)
    psum x1, waiting for transfers between devices, shards(): token_grad_sum = lax.psum(jnp.sum(grad_tokens, axis=0), ('tile', 'sample'))  128 us
    psum x1, waiting for transfers between devices, shards(): lax.psum((grad_tri_in_w, grad_tri_gate_w, grad_tri_out_w, grad_bias_w, gr...  99.3 us
    psum x1, blocking collectives, shards(): lax.psum((grad_tri_in_w, grad_tri_gate_w, grad_tri_out_w, grad_bias_w, gr...  68.7 us
    reduce_scatter x1, waiting for transfers between devices, shards(): lax.psum_scatter(bias_term.astype(jnp.bfloat16), 'sample', scatter_dimens...  51.9 us
    reduce_scatter x1, waiting for transfers between devices, shards(): lax.psum_scatter(bias_part, 'tile', scatter_dimension=1, tiled=True)  50.2 us
    reduce_scatter x1, waiting for transfers between devices, shards(): lax.psum_scatter(d_right_part.astype(jnp.bfloat16), 'tile', scatter_dimen...  43.4 us
    unnamed x132, local copies, waits for them, and re-layouts  41.8 us
    psum x1, waiting for transfers between devices, shards(): lax.psum(sums_part.astype(jnp.bfloat16), 'tile').astype(jnp.float32)  36.2 us
  transfers between devices with their start and end apart: 13, of which 11 were waited for; matrix products, arithmetic and copies ran while one was open for 13% of the time, Pallas kernels for 0%

commit v1 on v0

--- a/solution.py
+++ b/solution.py
@@ -1,12 +1,180 @@
+import functools
 import math
 
 import jax
 import jax.numpy as jnp
 from jax import lax
+from jax.experimental import pallas as pl
+from jax.experimental.pallas import tpu as pltpu
 from jax.sharding import PartitionSpec as P
 
 EPSILON = 1e-05
+N_TILE = 16
+N_SAMPLE = 8
+N_CHIP = 8
+MESH = pl.DeviceIdType.MESH
+BF16 = jnp.bfloat16
+F32 = jnp.float32
 HIGHEST = lax.Precision.HIGHEST
+
+
+def enter(t, s):
+    barrier = pltpu.get_barrier_semaphore()
+    for k in range(1, N_SAMPLE):
+        pl.semaphore_signal(
+            barrier, inc=1, device_id=(t, lax.rem(s + k, N_SAMPLE)), device_id_type=MESH
+        )
+    for k in range(1, N_TILE):
+        pl.semaphore_signal(
+            barrier, inc=1, device_id=(lax.rem(t + k, N_TILE), s), device_id_type=MESH
+        )
+    pl.semaphore_wait(barrier, N_SAMPLE + N_TILE - 2)
+
+
+def wait_bytes(ref, sem):
+    pltpu.make_async_copy(ref, ref, sem).wait()
+
+
+def send(src, dst, send_sem, recv_sem, t, s):
+    pltpu.make_async_remote_copy(
+        src, dst, send_sem, recv_sem, device_id=(t, s), device_id_type=MESH
+    ).start()
+
+
+def exchange_kernel(x, out, mid, send_sem, recv_sem, local_sem):
+    t, s = lax.axis_index("tile"), lax.axis_index("sample")
+    enter(t, s)
+    for k in range(1, N_SAMPLE):
+        d = lax.rem(s + k, N_SAMPLE)
+        send(x.at[:, d], mid.at[:, s], send_sem.at[0], recv_sem.at[0], t, d)
+    own = pltpu.make_async_copy(x.at[:, s], mid.at[:, s], local_sem)
+    own.start()
+    own.wait()
+    wait_bytes(mid.at[:, pl.ds(0, N_SAMPLE - 1)], recv_sem.at[0])
+    for k in range(1, N_TILE):
+        d = lax.rem(t + k, N_TILE)
+        send(mid.at[d], out.at[t], send_sem.at[1], recv_sem.at[1], d, s)
+    own = pltpu.make_async_copy(mid.at[t], out.at[t], local_sem)
+    own.start()
+    own.wait()
+    wait_bytes(out.at[pl.ds(0, N_TILE - 1)], recv_sem.at[1])
+    wait_bytes(mid.at[:, pl.ds(0, N_SAMPLE - 1)], send_sem.at[0])
+    wait_bytes(out.at[pl.ds(0, N_TILE - 1)], send_sem.at[1])
+
+
+def exchange(x, collective_id):
+    return pl.pallas_call(
+        exchange_kernel,
+        out_shape=jax.ShapeDtypeStruct(x.shape, x.dtype),
+        in_specs=[pl.BlockSpec(memory_space=pltpu.VMEM)],
+        out_specs=pl.BlockSpec(memory_space=pltpu.VMEM),
+        scratch_shapes=[
+            pltpu.VMEM(x.shape, x.dtype),
+            pltpu.SemaphoreType.DMA((2,)),
+            pltpu.SemaphoreType.DMA((2,)),
+            pltpu.SemaphoreType.DMA,
+        ],
+        compiler_params=pltpu.CompilerParams(
+            collective_id=collective_id, has_side_effects=True, vmem_limit_bytes=32 << 20
+        ),
+    )(x)
+
+
+def gather_kernel(x, out, send_sem, recv_sem, local_sem):
+    t, s = lax.axis_index("tile"), lax.axis_index("sample")
+    m, c = t // 2, lax.rem(t, 2)
+    other = m * 2 + 1 - c
+    enter(t, s)
+    own = pltpu.make_async_copy(x, out.at[m, c, s], local_sem)
+    own.start()
+    for k in range(1, N_SAMPLE):
+        send(x, out.at[m, c, s], send_sem.at[0], recv_sem.at[0], t, lax.rem(s + k, N_SAMPLE))
+    own.wait()
+    wait_bytes(out.at[m, c, pl.ds(0, N_SAMPLE - 1)], recv_sem.at[0])
+    block = out.at[m, c]
+    send(block, block, send_sem.at[1], recv_sem.at[N_CHIP], other, s)
+    for k in range(1, N_CHIP):
+        send(block, block, send_sem.at[1], recv_sem.at[k], lax.rem(m + k, N_CHIP) * 2 + c, s)
+    for k in range(1, N_CHIP):
+        arrived = out.at[lax.rem(m + N_CHIP - k, N_CHIP), c]
+        wait_bytes(arrived, recv_sem.at[k])
+        send(arrived, arrived, send_sem.at[1], recv_sem.at[N_CHIP], other, s)
+    wait_bytes(out.at[:, 0], recv_sem.at[N_CHIP])
+    wait_bytes(out.at[0, 0, pl.ds(0, N_SAMPLE - 1)], send_sem.at[0])
+    wait_bytes(out.at[:, 0], send_sem.at[1])
+    wait_bytes(out.at[pl.ds(0, N_CHIP - 1), 0], send_sem.at[1])
+
+
+def gather(x, collective_id):
+    return pl.pallas_call(
+        gather_kernel,
+        out_shape=jax.ShapeDtypeStruct((N_CHIP, 2, N_SAMPLE) + x.shape, x.dtype),
+        in_specs=[pl.BlockSpec(memory_space=pltpu.VMEM)],
+        out_specs=pl.BlockSpec(memory_space=pltpu.VMEM),
+        scratch_shapes=[
+            pltpu.SemaphoreType.DMA((2,)),
+            pltpu.SemaphoreType.DMA((N_CHIP + 1,)),
+            pltpu.SemaphoreType.DMA,
+        ],
+        compiler_params=pltpu.CompilerParams(
+            collective_id=collective_id, has_side_effects=True, vmem_limit_bytes=32 << 20
+        ),
+    )(x)
+
+
+def scatter_sum_kernel(x, out, pair_sum, by_chip, by_sample, send_sem, recv_sem):
+    t, s = lax.axis_index("tile"), lax.axis_index("sample")
+    m, c = t // 2, lax.rem(t, 2)
+    enter(t, s)
+    for k in range(1, N_CHIP + 1):
+        d = lax.rem(m + k, N_CHIP)
+        send(x.at[d, 1 - c], pair_sum.at[d], send_sem.at[0], recv_sem.at[k], m * 2 + 1 - c, s)
+    for k in range(1, N_CHIP + 1):
+        d = lax.rem(m + k, N_CHIP)
+        wait_bytes(pair_sum.at[d], recv_sem.at[k])
+        pair_sum[d] = (pair_sum[d].astype(F32) + x[d, c].astype(F32)).astype(x.dtype)
+        if k < N_CHIP:
+            send(
+                pair_sum.at[d],
+                by_chip.at[k - 1],
+                send_sem.at[1],
+                recv_sem.at[N_CHIP + k],
+                d * 2 + c,
+                s,
+            )
+    total = pair_sum[m].astype(F32)
+    for k in range(1, N_CHIP):
+        wait_bytes(by_chip.at[k - 1], recv_sem.at[N_CHIP + k])
+        total = total + by_chip[k - 1].astype(F32)
+    pair_sum[m] = total.astype(x.dtype)
+    for k in range(1, N_SAMPLE):
+        d = lax.rem(s + k, N_SAMPLE)
+        send(pair_sum.at[m, d], by_sample.at[k - 1], send_sem.at[2], recv_sem.at[0], t, d)
+    wait_bytes(by_sample, recv_sem.at[0])
+    out[...] = pair_sum[m, s].astype(F32) + jnp.sum(by_sample[...].astype(F32), axis=0)
+    wait_bytes(pair_sum, send_sem.at[0])
+    wait_bytes(by_chip, send_sem.at[1])
+    wait_bytes(by_sample, send_sem.at[2])
+
+
+def scatter_sum(x, collective_id):
+    block = x.shape[3:]
+    return pl.pallas_call(
+        scatter_sum_kernel,
+        out_shape=jax.ShapeDtypeStruct(block, F32),
+        in_specs=[pl.BlockSpec(memory_space=pltpu.VMEM)],
+        out_specs=pl.BlockSpec(memory_space=pltpu.VMEM),
+        scratch_shapes=[
+            pltpu.VMEM((N_CHIP, N_SAMPLE) + block, x.dtype),
+            pltpu.VMEM((N_CHIP - 1, N_SAMPLE) + block, x.dtype),
+            pltpu.VMEM((N_SAMPLE - 1,) + block, x.dtype),
+            pltpu.SemaphoreType.DMA((3,)),
+            pltpu.SemaphoreType.DMA((2 * N_CHIP,)),
+        ],
+        compiler_params=pltpu.CompilerParams(
+            collective_id=collective_id, has_side_effects=True, vmem_limit_bytes=32 << 20
+        ),
+    )(x)
 
 
 def norm_parts(values, axis):
@@ -56,18 +224,27 @@
     mask_rows = pair_mask.astype(jnp.float32)[None]
     gate_left = jax.nn.sigmoid(projected[0:hidden])
     gate_right = jax.nn.sigmoid(projected[2 * hidden : 3 * hidden])
-    left_local = (gate_left * projected[hidden : 2 * hidden] * mask_rows).astype(jnp.bfloat16)
-    right_local = (gate_right * projected[3 * hidden :] * mask_rows).astype(jnp.bfloat16)
-    left_panel, right_panel = (
-        lax.all_to_all(left_local, "sample", split_axis=0, concat_axis=2, tiled=True),
-        lax.all_to_all(right_local, "sample", split_axis=0, concat_axis=2, tiled=True),
-    )
-    right_all = lax.all_gather(right_panel, "tile", axis=1, tiled=True)
-    product_panel = jnp.einsum(
-        "cik,cjk->cij", left_panel, right_all, preferred_element_type=jnp.float32
-    ).astype(jnp.bfloat16)
-    product = lax.all_to_all(product_panel, "sample", split_axis=2, concat_axis=0, tiled=True)
-    normed_p, inverse_p = norm_parts(product.astype(jnp.float32), 0)
+    rows, columns = pair_mask.shape
+    blocks = (N_TILE, N_SAMPLE)
+    left_local = (gate_left * projected[hidden : 2 * hidden] * mask_rows).astype(BF16)
+    right_local = (gate_right * projected[3 * hidden :] * mask_rows).astype(BF16)
+    halves = jnp.stack([left_local, right_local], axis=1).astype(F32)
+    halves = exchange(halves.reshape(blocks + (8, 128)), 0)
+    panels = (
+        halves.reshape(blocks + (2, rows, columns))
+        .astype(BF16)
+        .transpose(2, 0, 3, 1, 4)
+        .reshape(2, N_TILE * rows, N_SAMPLE * columns)
+    )
+    left_panel, right_panel = panels[0], panels[1]
+    product_panel = jnp.dot(left_panel, right_panel.T, preferred_element_type=F32).astype(BF16)
+    product_blocks = (
+        product_panel.reshape(N_TILE, rows, N_SAMPLE, columns)
+        .transpose(0, 2, 1, 3)
+        .reshape(blocks + (4, 128))
+    )
+    product = exchange(product_blocks.astype(F32), 1).reshape(hidden, rows, columns)
+    normed_p, inverse_p = norm_parts(product, 0)
     normed_pb = normed_p.astype(jnp.bfloat16)
     linear = jnp.einsum("cij,cz->ijz", normed_pb, tri_out_w, preferred_element_type=jnp.float32)
     tri_gate = jax.nn.sigmoid(
@@ -79,18 +256,20 @@
     bias_local = jnp.einsum(
         "ijz,zh->hij", normed_nb, bias_w, preferred_element_type=jnp.float32
     ).astype(jnp.bfloat16)
-    bias_rowblock = lax.all_gather(bias_local, "sample", axis=2, tiled=True)
-    bias_all = lax.all_gather(bias_rowblock, "tile", axis=1, tiled=True)
-    atom_pre = jnp.dot(atom_feats, atom_w, preferred_element_type=jnp.float32)
-    atom_act = jax.nn.silu(atom_pre)
+    bias_all = (
+        gather(bias_local.reshape(head_count, rows * columns), 2)
+        .reshape(N_TILE, N_SAMPLE, head_count, rows, columns)
+        .transpose(2, 0, 3, 1, 4)
+        .reshape(head_count, N_TILE * rows, N_SAMPLE * columns)
+    )
+    every_feat = lax.all_gather(atom_feats, "tile", axis=0, tiled=True)
+    every_atom = lax.all_gather(atom_to_token, "tile", axis=0, tiled=True)
+    atom_pre = jnp.dot(every_feat, atom_w, preferred_element_type=jnp.float32)
+    atom_act = jax.nn.silu(atom_pre).astype(BF16)
     token_ids = jnp.arange(total_tokens, dtype=jnp.int32)
-    one_hot = (atom_to_token[:, None] == token_ids[None, :]).astype(jnp.float32)
-    sums_part = jnp.einsum("an,ad->nd", one_hot, atom_act, precision=HIGHEST)
-    counts_part = jnp.sum(one_hot, axis=0)
-    token_sums, token_counts = (
-        lax.psum(sums_part.astype(jnp.bfloat16), "tile").astype(jnp.float32),
-        lax.psum(counts_part.astype(jnp.bfloat16), "tile").astype(jnp.float32),
-    )
+    one_hot = (token_ids[:, None] == every_atom[None, :]).astype(BF16)
+    token_sums = jnp.dot(one_hot, atom_act, preferred_element_type=F32)
+    token_counts = jnp.sum(one_hot.astype(F32), axis=1)
     token_cond = token_sums / token_counts[:, None]
     token_state_rows = tokens.astype(jnp.float32) + token_cond[None]
     normed_h, inverse_h = norm_parts(token_state_rows, 2)
@@ -167,12 +346,13 @@
         .reshape(sample_count, total_tokens, token_width)
     )
     bias_term = jnp.sum(d_scores, axis=0)
-    bias_part = lax.psum_scatter(
-        bias_term.astype(jnp.bfloat16), "sample", scatter_dimension=2, tiled=True
-    )
-    bias_grad = lax.psum_scatter(bias_part, "tile", scatter_dimension=1, tiled=True).astype(
-        jnp.float32
-    )
+    bias_blocks = (
+        bias_term.astype(BF16)
+        .reshape(head_count, N_CHIP, 2, rows, N_SAMPLE, columns)
+        .transpose(1, 2, 4, 0, 3, 5)
+        .reshape(N_CHIP, 2, N_SAMPLE, head_count, rows * columns)
+    )
+    bias_grad = scatter_sum(bias_blocks, 3).reshape(head_count, rows, columns)
     every_gradient = jnp.concatenate([d_query, d_gate, d_key, d_value], axis=2)
     normalized_hidden_gradient = jnp.einsum(
         "xqu,bu->xqb", every_gradient, attention_input_weight, preferred_element_type=jnp.float32
@@ -186,13 +366,12 @@
     grad_tokens = token_output_cotangent.astype(jnp.float32) + norm_back(
         normed_h, inverse_h, normalized_hidden_gradient, 2
     )
-    token_grad_sum = lax.psum(jnp.sum(grad_tokens, axis=0), ("tile", "sample"))
-    cond_grad = token_grad_sum / token_counts[:, None]
-    d_act = jnp.einsum("an,nd->ad", one_hot, cond_grad, precision=HIGHEST) * silu_slope(atom_pre)
-    first_copy = (lax.axis_index("sample") == 0).astype(jnp.float32)
-    grad_atom_w = (
-        jnp.einsum("ac,ad->cd", atom_feats.astype(jnp.float32), d_act, precision=HIGHEST)
-        * first_copy
+    cond_grad = (jnp.sum(grad_tokens, axis=0) / token_counts[:, None]).astype(BF16)
+    d_act = lax.dot_general(
+        one_hot, cond_grad, (((0,), (0,)), ((), ())), preferred_element_type=F32
+    ) * silu_slope(atom_pre)
+    grad_atom_w = lax.dot_general(
+        every_feat, d_act.astype(BF16), (((0,), (0,)), ((), ())), preferred_element_type=F32
     )
     d_normed_n = jnp.einsum("hij,zh->ijz", bias_grad, bias_w.astype(jnp.float32), precision=HIGHEST)
     grad_bias_w = jnp.einsum(
@@ -206,28 +385,29 @@
     )
     d_normed_p = jnp.einsum("ijz,cz->cij", d_linear, tri_out_w, preferred_element_type=jnp.float32)
     d_product = norm_back(normed_p, inverse_p, d_normed_p, 0).astype(jnp.bfloat16)
-    d_product_panel = lax.all_to_all(d_product, "sample", split_axis=0, concat_axis=2, tiled=True)
-    d_left_panel = jnp.einsum(
-        "cij,cjk->cik", d_product_panel, right_all, preferred_element_type=jnp.float32
-    ).astype(jnp.bfloat16)
-    d_right_part = jnp.einsum(
-        "cij,cik->cjk", d_product_panel, left_panel, preferred_element_type=jnp.float32
-    )
-    d_right_panel = lax.psum_scatter(
-        d_right_part.astype(jnp.bfloat16), "tile", scatter_dimension=1, tiled=True
-    )
-    d_left, d_right = (
-        lax.all_to_all(d_left_panel, "sample", split_axis=2, concat_axis=0, tiled=True),
-        lax.all_to_all(d_right_panel, "sample", split_axis=2, concat_axis=0, tiled=True),
-    )
-    d_left_f = d_left.astype(jnp.float32)
-    d_right_f = d_right.astype(jnp.float32)
+    d_product_panel = (
+        exchange(d_product.astype(F32).reshape(blocks + (4, 128)), 4)
+        .reshape(blocks + (rows, columns))
+        .astype(BF16)
+        .transpose(0, 2, 1, 3)
+        .reshape(N_TILE * rows, N_SAMPLE * columns)
+    )
+    d_left_panel = jnp.dot(d_product_panel, right_panel, preferred_element_type=F32)
+    d_right_panel = jnp.dot(d_product_panel.T, left_panel, preferred_element_type=F32)
+    d_halves = (
+        jnp.stack([d_left_panel, d_right_panel])
+        .reshape(2, N_TILE, rows, N_SAMPLE, columns)
+        .transpose(1, 3, 0, 2, 4)
+        .reshape(blocks + (8, 128))
+    )
+    d_halves = exchange(d_halves, 5).reshape(hidden, 2, rows, columns)
+    d_left, d_right = d_halves[:, 0], d_halves[:, 1]
     d_proj = jnp.concatenate(
         [
-            d_left_f * projected[hidden : 2 * hidden] * mask_rows * gate_left * (1.0 - gate_left),
-            d_left_f * gate_left * mask_rows,
-            d_right_f * projected[3 * hidden :] * mask_rows * gate_right * (1.0 - gate_right),
-            d_right_f * gate_right * mask_rows,
+            d_left * projected[hidden : 2 * hidden] * mask_rows * gate_left * (1.0 - gate_left),
+            d_left * gate_left * mask_rows,
+            d_right * projected[3 * hidden :] * mask_rows * gate_right * (1.0 - gate_right),
+            d_right * gate_right * mask_rows,
         ],
         axis=0,
     ).astype(jnp.bfloat16)
@@ -239,20 +419,17 @@
         "cij,zc->ijz", d_proj, tri_in_w, preferred_element_type=jnp.float32
     ) + jnp.einsum("ijy,zy->ijz", d_gate_pre, tri_gate_w, preferred_element_type=jnp.float32)
     grad_pair = d_next + norm_back(normed_z, inverse_z, d_normed_z, 2)
-    summed = tuple(
-        lax.psum(
-            (
-                grad_tri_in_w,
-                grad_tri_gate_w,
-                grad_tri_out_w,
-                grad_bias_w,
-                grad_atom_w,
-                attention_input_weight_gradient,
-                attention_output_weight_gradient,
-            ),
-            ("tile", "sample"),
-        )
-    )
+    axes = ("tile", "sample")
+    grad_in_w, grad_out_w = lax.psum(
+        (
+            attention_input_weight_gradient.astype(BF16),
+            attention_output_weight_gradient.astype(BF16),
+        ),
+        axes,
+    )
+    summed = lax.psum(
+        (grad_tri_in_w, grad_tri_gate_w, grad_tri_out_w, grad_bias_w, grad_atom_w), axes
+    ) + (grad_in_w.astype(F32), grad_out_w.astype(F32))
     return (pair_next, token_output_rows, grad_pair, grad_tokens) + summed
 
 

time: 888 us -> 699 us (0.79)
  waiting for transfers between devices: 464 us -> 222 us
  Pallas kernels: 0 us -> 122 us
  blocking collectives: 153 us -> 102 us
  starting transfers between devices: 29.2 us -> 0.08 us
  local copies, waits for them, and re-layouts: 105 us -> 117 us
  matrix products: 90.3 us -> 80.5 us
    reduce_scatter x3 -> x0, waiting for transfers between devices: 146 us -> none  [the longest x1 51.9 us: shards(): lax.psum_scatter(bias_term.astype(jnp.bfloat16), 'sample', scatter_dimens...]
    pallas_call x0 -> x6, Pallas kernels: none -> 122 us  [the longest x4 75.6 us: exchange(): pl.pallas_call(exchange_kernel, out_shape=jax.ShapeDtypeStruct(x.shape, x...]
    all_gather x2 -> x0, waiting for transfers between devices: 41 us -> none  [the longest x1 20.9 us: shards(): bias_all = lax.all_gather(bias_rowblock, 'tile', axis=1, tiled=True)]
    convert_element_type x1 -> x4, local copies, waits for them, and re-layouts: 4.96 us -> 43.4 us  [shards(): bias_all.astype(jnp.float32)[None]]
    psum x1, waiting for transfers between devices: 99.3 us -> 63.1 us  [shards(): lax.psum((grad_tri_in_w, grad_tri_gate_w, grad_tri_out_w, grad_bias_w, gr...]
    psum x1 -> x0, blocking collectives: 33.4 us -> none  [shards(): lax.psum(counts_part.astype(jnp.bfloat16), 'tile').astype(jnp.float32)]
    unnamed x132 -> x158, local copies, waits for them, and re-layouts: 41.8 us -> 11.9 us
    all_to_all x5 -> x0, starting transfers between devices: 28.4 us -> none  [the longest x1 6.84 us: shards(): lax.all_to_all(d_product, 'sample', split_axis=0, concat_axis=2, tiled=True)]
  transfers between devices with their start and end apart: 13 -> 2, of which waited for: 11 -> 2; matrix products, arithmetic and copies ran while one was open for 13% -> 3% of each run, Pallas kernels for 0% -> 0%
where the time goes in v1:
time: 699 us; the launch traced here: 688 us
  waiting for transfers between devices  222 us (32%)
  Pallas kernels  122 us (17%)
  local copies, waits for them, and re-layouts  117 us (17%)
  blocking collectives  102 us (15%)
  matrix products  80.5 us (12%)
  other arithmetic  27.4 us (4%)
  between operations  15.6 us (2%)
    psum x1, waiting for transfers between devices, shards(): lax.psum((attention_input_weight_gradient.astype(BF16), attention_output_...  159 us
    pallas_call x4, Pallas kernels, exchange(): pl.pallas_call(exchange_kernel, out_shape=jax.ShapeDtypeStruct(x.shape, x...  75.6 us
    psum x1, blocking collectives, shards(): lax.psum((grad_tri_in_w, grad_tri_gate_w, grad_tri_out_w, grad_bias_w, gr...  64.8 us
    psum x1, waiting for transfers between devices, shards(): lax.psum((grad_tri_in_w, grad_tri_gate_w, grad_tri_out_w, grad_bias_w, gr...  63.1 us
    convert_element_type x4, local copies, waits for them, and re-layouts, shards(): bias_all.astype(jnp.float32)[None]  43.4 us
    pallas_call x1, Pallas kernels, gather(): pl.pallas_call(gather_kernel, out_shape=jax.ShapeDtypeStruct((N_CHIP, 2,...  23.3 us
    pallas_call x1, Pallas kernels, scatter_sum(): pl.pallas_call(scatter_sum_kernel, out_shape=jax.ShapeDtypeStruct(block,...  23.2 us
    all_gather x1, blocking collectives, shards(): every_atom = lax.all_gather(atom_to_token, 'tile', axis=0, tiled=True)  19.5 us
  transfers between devices with their start and end apart: 2, of which 2 were waited for; matrix products, arithmetic and copies ran while one was open for 3% of the time, Pallas kernels for 0%

profile of v1, /device:TPU:1, one launch (start us, length us, event | category | flops | bytes accessed | tf_op | source)
XLA Modules:
  0.0 688.1 jit_solution(6630179168357997427)
XLA Ops:
  17.7 23.4 %shard_map.221 = f32[16,8,8,128]{3,2,1,0:T(8,128)S(1)} custom-call(f32[16,8,8,128]{3,2,1,0:T(8,128)S(1)} %reshape.248.x), custom_call_target="tpu_custom_call" | custom-call | tf_op jit(solution)/shard_map/pallas_call | solution.py:66
  44.5 14.7 %shard_map.222 = f32[16,8,4,128]{3,2,1,0:T(4,128)S(1)} custom-call(f32[16,8,4,128]{3,2,1,0:T(4,128)S(1)} %reshape.249.x), custom_call_target="tpu_custom_call" | custom-call | tf_op jit(solution)/shard_map/pallas_call | solution.py:66
  62.7 23.3 %shard_map.223 = bf16[8,2,8,16,512]{4,3,2,1,0:T(8,128)(2,1)S(1)} custom-call(bf16[16,512]{1,0:T(8,128)(2,1)S(1)} %reshape.233.x), custom_call_target="tpu_custom_call" | custom-call | tf_op jit(solution)/shard_map/pallas_call | solution.py:109
  86.1 8.1 %reshape.254 = f32[16,8,16,16,32]{4,3,2,1,0:T(8,128)} reshape(bf16[8,2,8,16,512]{4,3,2,1,0:T(8,128)(2,1)S(1)} %shard_map.223) | data formatting | bytes 6291456 | tf_op jit(solution)/shard_map/convert_element_type | solution.py:302
  94.1 17.7 %copy.213 = f32[16,8,16,16,32]{4,1,3,0,2:T(8,128)} copy(f32[16,8,16,16,32]{4,3,2,1,0:T(8,128)} %reshape.254) | data formatting | bytes 8388608 | tf_op jit(solution)/shard_map/convert_element_type | solution.py:302
  111.9 12.2 %reshape.250 = f32[16,256,256]{2,1,0:T(8,128)} reshape(f32[16,16,16,8,32]{4,3,2,1,0:T(8,128)} %bitcast.204) | data formatting | bytes 8388608 | tf_op jit(solution)/shard_map/convert_element_type | solution.py:302
  124.1 5.4 copy.167
  129.5 19.5 %all-gather = s32[16,1,128]{2,1,0:T(1,128)S(1)} all-gather(s32[1,1,128]{2,1,0:T(1,128)S(1)} %bitcast.235), channel_id=1, replica_groups=mesh['tile'=16,'sample'=8] {'tile'}, dimensions={0}, use_global_device_ids=true | all-gather | bytes 8704 | tf_op jit(solution)/shard_map/all_gather | solution.py:266
  149.3 18.0 %all_gather.7 = bf16[2048,128]{1,0:T(8,128)(2,1)S(1)} all-gather(bf16[128,128]{1,0:T(8,128)(2,1)S(1)} %copy-done.63), channel_id=1, replica_groups=mesh['tile'=16,'sample'=8] {'tile'}, dimensions={0}, use_global_device_ids=true | all-gather | bytes 557056 | tf_op jit(solution)/shard_map/all_gather | solution.py:265
  181.7 7.4 %fusion.119 = (f32[2,16,256]{2,1,0:T(8,128)}, f32[2,16,256,256]{2,3,1,0:T(8,128)}) fusion(f32[16,256,256]{1,2,0:T(8,128)} %copy.167, bf16[2,256,16,48]{1,3,2,0:T(8,128)(2,1)S(1)} %bitcast.208, bf16[2,256,16,48]{1,3,2,0:T(8,128)(2,1)S(1)} %bitcast.210), kind=kOutput, calls=%fused_computation.184 | convolution fusion | flops 209715456 | bytes 14188544 | tf_op jit(solution)/shard_map/sub | solution.py:305
  202.7 5.8 fusion.25
  226.1 6.2 convert_element_type.201
  232.4 9.1 %copy.172 = bf16[8,2,8,16,16,32]{5,4,3,2,1,0:T(8,128)(2,1)} copy(bf16[8,2,8,16,16,32]{5,2,4,1,0,3:T(8,128)(2,1)} %bitcast.205) | data formatting | bytes 4194304 | tf_op jit(solution)/shard_map/transpose | solution.py:352
  241.5 10.9 %reshape.236.x = bf16[8,2,8,16,512]{4,3,2,1,0:T(8,128)(2,1)S(1)} reshape(bf16[8,2,8,16,16,32]{5,4,3,2,1,0:T(8,128)(2,1)} %copy.172) | data formatting | bytes 4194304 | tf_op jit(solution)/shard_map/reshape | solution.py:353
  252.5 23.2 %shard_map.224 = f32[16,512]{1,0:T(8,128)S(1)} custom-call(bf16[8,2,8,16,512]{4,3,2,1,0:T(8,128)(2,1)S(1)} %reshape.236.x), custom_call_target="tpu_custom_call" | custom-call | tf_op jit(solution)/shard_map/pallas_call | solution.py:162
  283.2 17.4 %shard_map.225 = f32[16,8,4,128]{3,2,1,0:T(4,128)S(1)} custom-call(f32[16,8,4,128]{3,2,1,0:T(4,128)S(1)} %reshape.252.x), custom_call_target="tpu_custom_call" | custom-call | tf_op jit(solution)/shard_map/pallas_call | solution.py:66
  308.7 6.2 fusion.109
  317.7 7.5 %fusion.28 = f32[128,768]{0,1:T(8,128)} fusion(bf16[2048,128]{1,0:T(8,128)(2,1)S(1)} %copy-done.16, f32[2048,768]{1,0:T(8,128)} %copy-done.3, s32[2048]{0:T(1024)} %bitcast.234, f32[256,768]{1,0:T(8,128)} %get-tuple-element.80, f32[256]{0:T(256)} %copy-done.68), kind=kOutput, calls=%fused_computation.54 | convolution fusion | flops 1223032832 | bytes 8004608 | tf_op jit(solution)/shard_map/dot_general | solution.py:373
  330.1 20.2 %shard_map.226 = f32[16,8,8,128]{3,2,1,0:T(8,128)S(1)} custom-call(f32[16,8,8,128]{3,2,1,0:T(8,128)S(1)} %reshape.243.x), custom_call_target="tpu_custom_call" | custom-call | tf_op jit(solution)/shard_map/pallas_call | solution.py:66
  362.8 7.0 %bitcast_convert_fusion = bf16[768,3072]{1,0:T(8,128)(2,1)} fusion(bf16[2,256,768]{2,1,0:T(8,128)(2,1)} %copy.188, bf16[2,256,768]{2,1,0:T(8,128)(2,1)} %copy.187, bf16[2,256,768]{2,1,0:T(8,128)(2,1)} %get-tuple-element.86, bf16[2,256,768]{2,1,0:T(8,128)(2,1)} %copy.186, bf16[2,256,768]{2,1,0:T(8,128)(2,1)S(1)} %copy-done.6, f32[2,256]{1,0:T(2,128)} %copy-done.60, ...), kind=kOutput, calls=%fused_computation.2 | convolution fusion | flops 2432827392 | bytes 9441280 | tf_op jit(solution)/shard_map/jol,jot->lt/dot_general | solution.py:360
  373.5 64.8 %psum.52 = f32[128,16]{0,1:T(8,128)} all-reduce(f32[128,16]{0,1:T(8,128)} %convolution_bitcast_fusion.7), channel_id=1, replica_groups=mesh['tile'=16,'sample'=8] {'tile','sample'}, use_global_device_ids=true, to_apply=%region_24.25 | all-reduce | flops 2048 | bytes 16384 | tf_op jit(solution)/shard_map/psum | solution.py:430
  445.5 63.1 %all-reduce.5.cloned.1.call-done = (f32[128,512]{1,0:T(8,128)}, f32[128,128]{1,0:T(8,128)}, f32[128,128]{1,0:T(8,128)}, f32[128,768]{0,1:T(8,128)}) async-done(((f32[128,512]{1,0:T(8,128)}, f32[128,128]{1,0:T(8,128)}, f32[128,128]{1,0:T(8,128)}, f32[128,768]{0,1:T(8,128)}), (f32[128,512]{1,0:T(8,128)}, f32[128,128]{1,0:T(8,128)}, f32[128,128]{1,0:T(8,128)}, ...) | async-done | bytes 786448 | tf_op jit(solution)/shard_map/psum | solution.py:430
  510.4 159.4 %all-reduce.7.cloned.1.call-done = (bf16[768,3072]{1,0:T(8,128)(2,1)}, bf16[768,768]{1,0:T(8,128)(2,1)}) async-done(((bf16[768,3072]{1,0:T(8,128)(2,1)}, bf16[768,768]{1,0:T(8,128)(2,1)}), (bf16[768,3072]{1,0:T(8,128)(2,1)}, bf16[768,768]{1,0:T(8,128)(2,1)})) %all-reduce.7.cloned.1.call-update) | async-done | bytes 5898256 | tf_op jit(solution)/shard_map/psum | solution.py:423
  669.8 7.5 %convert_element_type.219 = f32[768,3072]{1,0:T(8,128)} convert(bf16[768,3072]{1,0:T(8,128)(2,1)} %get-tuple-element.78) | non-fusion elementwise | flops 2359296 | bytes 14155776 | tf_op jit(solution)/shard_map/convert_element_type | solution.py:432
  (264 shorter events, 114.4 us)
Async XLA Ops:
  7.2 189.3 %copy-start = (bf16[768,768]{1,0:T(8,128)(2,1)S(1)}, bf16[768,768]{1,0:T(8,128)(2,1)}, u32[]{:S(2)}) copy-start(bf16[768,768]{1,0:T(8,128)(2,1)} %param.25) | copy-start | bytes 3538948
  7.2 501.3 %all-reduce.5.cloned.1.call-start = ((), (), s32[]{:S(2)}) async-start(), calls=%async_computation | async-start | bytes 1572864 | tf_op jit(solution)/shard_map/psum | solution.py:430
  8.4 52.4 %copy-start.38 = (f32[16,32]{1,0:T(8,128)}, f32[16,32]{1,0:T(8,128)S(1)}, u32[]{:S(2)}) copy-start(f32[16,32]{1,0:T(8,128)S(1)} %broadcast_multiply_fusion.7) | copy-start | bytes 6148
  9.6 51.2 %copy-start.51 = (f32[16,32]{1,0:T(8,128)}, f32[16,32]{1,0:T(8,128)S(1)}, u32[]{:S(2)}) copy-start(f32[16,32]{1,0:T(8,128)S(1)} %add_rsqrt_fusion.1) | copy-start | bytes 6148
  43.9 16.5 %copy-start.49 = (bf16[128,128]{1,0:T(8,128)(2,1)S(1)}, bf16[128,128]{1,0:T(8,128)(2,1)}, u32[]{:S(2)}) copy-start(bf16[128,128]{1,0:T(8,128)(2,1)} %param.18) | copy-start | bytes 98308
  44.1 16.6 %copy-start.17 = (bf16[16,32,128]{2,1,0:T(8,128)(2,1)S(1)}, bf16[16,32,128]{2,1,0:T(8,128)(2,1)}, u32[]{:S(2)}) copy-start(bf16[16,32,128]{2,1,0:T(8,128)(2,1)} %param.14) | copy-start | bytes 393220
  44.1 16.6 %copy-start.65 = (bf16[128,128]{1,0:T(8,128)(2,1)S(1)}, bf16[128,128]{1,0:T(8,128)(2,1)}, u32[]{:S(2)}) copy-start(bf16[128,128]{1,0:T(8,128)(2,1)} %param.17) | copy-start | bytes 98308
  44.5 17.7 %copy-start.66 = (bf16[128,16]{0,1:T(8,128)(2,1)S(1)}, bf16[128,16]{0,1:T(8,128)(2,1)}, u32[]{:S(2)}) copy-start(bf16[128,16]{0,1:T(8,128)(2,1)} %param.19) | copy-start | bytes 12292
  124.1 25.2 %copy-start.63 = (bf16[128,128]{1,0:T(8,128)(2,1)S(1)}, bf16[128,128]{1,0:T(8,128)(2,1)}, u32[]{:S(2)}) copy-start(bf16[128,128]{1,0:T(8,128)(2,1)} %param.20) | copy-start | bytes 98308
  124.1 44.1 %copy-start.39 = (bf16[128,768]{1,0:T(8,128)(2,1)S(1)}, bf16[128,768]{1,0:T(8,128)(2,1)}, u32[]{:S(2)}) copy-start(bf16[128,768]{1,0:T(8,128)(2,1)} %param.22) | copy-start | bytes 589828
  149.0 20.1 %copy-start.64 = (s32[16,1,128]{2,1,0:T(1,128)}, s32[16,1,128]{2,1,0:T(1,128)S(1)}, u32[]{:S(2)}) copy-start(s32[16,1,128]{2,1,0:T(1,128)S(1)} %all-gather) | copy-start | bytes 24580
  149.3 19.8 %copy-start.68 = (f32[256]{0:T(256)}, f32[256]{0:T(256)S(1)}, u32[]{:S(2)}) copy-start(f32[256]{0:T(256)S(1)} %convert_reduce_fusion) | copy-start | bytes 3076
  178.8 10.3 %copy-start.10 = (bf16[2,256,768]{1,2,0:T(8,128)(2,1)}, bf16[2,256,768]{1,2,0:T(8,128)(2,1)S(1)}, u32[]{:S(2)}) copy-start(bf16[2,256,768]{1,2,0:T(8,128)(2,1)S(1)} %copy.163) | copy-start | bytes 2359300
  202.7 11.0 %slice-start = ((s8[8388608]{0:T(1024)(128)(4,1)}), s8[4194304]{0:T(1024)(128)(4,1)S(1)}, s32[]{:S(2)}) async-start(s8[8388608]{0:T(1024)(128)(4,1)} %bitcast.206), calls=%async_computation.2 | async-start | bytes 8388608
  241.5 34.3 %copy-start.67 = (bf16[128,16]{0,1:T(8,128)(2,1)S(1)}, bf16[128,16]{0,1:T(8,128)(2,1)}, u32[]{:S(2)}) copy-start(bf16[128,16]{0,1:T(8,128)(2,1)} %param.19) | copy-start | bytes 12292
  241.5 35.9 %copy-start.36 = (bf16[16,32,128]{2,1,0:T(8,128)(2,1)S(1)}, bf16[16,32,128]{2,1,0:T(8,128)(2,1)}, u32[]{:S(2)}) copy-start(bf16[16,32,128]{2,1,0:T(8,128)(2,1)} %param.26) | copy-start | bytes 393220
  252.4 27.2 %copy-start.42 = (f32[16,32]{1,0:T(8,128)S(1)}, f32[16,32]{1,0:T(8,128)}, u32[]{:S(2)}) copy-start(f32[16,32]{1,0:T(8,128)} %copy-done.41) | copy-start | bytes 6148
  252.5 27.2 %copy-start.44 = (f32[16,32]{1,0:T(8,128)S(1)}, f32[16,32]{1,0:T(8,128)}, u32[]{:S(2)}) copy-start(f32[16,32]{1,0:T(8,128)} %copy-done.43) | copy-start | bytes 6148
  252.5 29.1 %copy-start.50 = (bf16[128,128]{1,0:T(8,128)(2,1)S(1)}, bf16[128,128]{1,0:T(8,128)(2,1)}, u32[]{:S(2)}) copy-start(bf16[128,128]{1,0:T(8,128)(2,1)} %param.18) | copy-start | bytes 98308
  277.4 23.2 %copy-start.53 = (f32[16,32]{1,0:T(8,128)}, f32[16,32]{1,0:T(8,128)S(1)}, u32[]{:S(2)}) copy-start(f32[16,32]{1,0:T(8,128)S(1)} %get-tuple-element.117) | copy-start | bytes 6148
  277.4 23.2 %copy-start.54 = (f32[16,32]{1,0:T(8,128)}, f32[16,32]{1,0:T(8,128)S(1)}, u32[]{:S(2)}) copy-start(f32[16,32]{1,0:T(8,128)S(1)} %get-tuple-element.118) | copy-start | bytes 6148
  360.1 9.6 %copy-start.45 = (bf16[128,16,32]{0,2,1:T(8,128)(2,1)}, bf16[128,16,32]{0,2,1:T(8,128)(2,1)S(1)}, u32[]{:S(2)}) copy-start(bf16[128,16,32]{0,2,1:T(8,128)(2,1)S(1)} %get-tuple-element.94) | copy-start | bytes 393220
  362.7 307.1 %all-reduce.7.cloned.1.call-start = ((), (), s32[]{:S(2)}) async-start(), calls=%async_computation.1 | async-start | bytes 11796480 | tf_op jit(solution)/shard_map/psum | solution.py:423
  372.5 68.7 %copy-start.20 = (f32[16,32,128]{2,1,0:T(8,128)S(1)}, f32[16,32,128]{2,1,0:T(8,128)}, u32[]{:S(2)}) copy-start(f32[16,32,128]{2,1,0:T(8,128)} %copy-done.19) | copy-start | bytes 786436
  (54 other events, 232.0 us)
Sparse Core Ops, SparseCore 0:
  362.8 145.6 all-reduce.4
  514.2 155.6 all-reduce.6
